TPU v7x, 32 devices: a whole 2x2x4 slice. The times are simulated.
32 devices in a mesh: ctx: 16 (over z, x, core), head: 2 (over y).
Axes of the slice: x: 2, y: 2, z: 4, core: 2. Of those that a mesh axis runs over, the one named last changes fastest.
Arguments:
- queries: bfloat16 [6144, 4096], P('ctx', 'head'), may hold values from -8 to 8
- keys: bfloat16 [6144, 4096], P('ctx', 'head'), may hold values from -8 to 8
- values: bfloat16 [6144, 4096], P('ctx', 'head'), may hold values from -6 to 6
- rates: bfloat16 [6144, 8], P('ctx', 'head'), may hold values from 0.00025367737 to 0.0025482178
- fast_gate: bfloat16 [8, 512, 512], P('head'), may hold values from -0.25 to 0.25
- fast_up: bfloat16 [8, 512, 512], P('head'), may hold values from -0.25 to 0.25
- fast_down: bfloat16 [8, 512, 512], P('head'), may hold values from -0.25 to 0.25
Outputs:
- mixed: bfloat16 [6144, 4096], P('ctx', 'head')
All inputs are finite; a program needn't handle non-finite values.
Results may differ from a plain program's by a relative error of at most 0.009.
Values may be sent and summed in bfloat16 or wider, within the bound.
A program may use at most 128 MiB of HBM per device.

v0:
```python
import jax
import jax.numpy as jnp
from jax import lax
from jax.sharding import PartitionSpec as P

ATT_DIM = 128
FAST_DIM = 512
WINDOW = 1024


def shifted(value, axis, by):
    length = lax.axis_size(axis)
    pairs = [(i, i + by) for i in range(length) if 0 <= i + by < length]
    return lax.ppermute(value, axis, pairs)


def silu_parts(pre_act):
    sigmoid = jax.nn.sigmoid(pre_act)
    return (pre_act * sigmoid, sigmoid * (1.0 + pre_act * (1.0 - sigmoid)))


def fast_gradients(key_rows, value_rows, rate_column, gate, upward, downward):
    gate_pre = jnp.dot(key_rows, gate.T, preferred_element_type=jnp.float32)
    up_pre = jnp.dot(key_rows, upward.T, preferred_element_type=jnp.float32)
    activated, slope = silu_parts(gate_pre)
    hidden = (activated * up_pre).astype(jnp.bfloat16)
    out_grad = (-rate_column.astype(jnp.float32)[:, None] * value_rows.astype(jnp.float32)).astype(
        jnp.bfloat16
    )
    hidden_grad = jnp.dot(out_grad, downward, preferred_element_type=jnp.float32)
    gate_grad = (hidden_grad * up_pre * slope).astype(jnp.bfloat16)
    up_grad = (hidden_grad * activated).astype(jnp.bfloat16)
    grad_gate = jnp.dot(gate_grad.T, key_rows, preferred_element_type=jnp.float32)
    grad_up = jnp.dot(up_grad.T, key_rows, preferred_element_type=jnp.float32)
    grad_down = jnp.dot(out_grad.T, hidden, preferred_element_type=jnp.float32)
    return jnp.stack([grad_gate, grad_up, grad_down])


def head_gradients(key_rows, value_rows, rate_rows, gates, uppers, downers):
    results = []
    for head_index in range(gates.shape[0]):
        first = head_index * FAST_DIM
        results.append(
            fast_gradients(
                key_rows[:, first : first + FAST_DIM],
                value_rows[:, first : first + FAST_DIM],
                rate_rows[:, head_index],
                gates[head_index],
                uppers[head_index],
                downers[head_index],
            )
        )
    return jnp.stack(results)


def renormalize(weights, gradient):
    initial = weights.astype(jnp.float32)
    moved = initial - gradient
    target = jnp.sqrt(jnp.sum(initial * initial, axis=-1, keepdims=True))
    current = jnp.sqrt(jnp.sum(moved * moved, axis=-1, keepdims=True) + 1e-06)
    return (moved * (target / current)).astype(jnp.bfloat16)


def apply_fast(query_rows, gate, upward, downward):
    gate_pre = jnp.dot(query_rows, gate.T, preferred_element_type=jnp.float32)
    up_pre = jnp.dot(query_rows, upward.T, preferred_element_type=jnp.float32)
    activated, slope = silu_parts(gate_pre)
    applied = (activated * up_pre).astype(jnp.bfloat16)
    return jnp.dot(applied, downward.T, preferred_element_type=jnp.float32)


def head_outputs(query_rows, fresh):
    pieces = []
    for head_index in range(fresh.shape[0]):
        first = head_index * FAST_DIM
        pieces.append(
            apply_fast(
                query_rows[:, first : first + FAST_DIM],
                fresh[head_index, 0],
                fresh[head_index, 1],
                fresh[head_index, 2],
            )
        )
    return jnp.concatenate(pieces, axis=1)


def window_attention(queries, window_keys, window_values, offset, span):
    rows_here = queries.shape[0]
    width = queries.shape[1]
    length = window_keys.shape[0]
    scale = ATT_DIM ** (-0.5)
    row_ids = jnp.arange(rows_here, dtype=jnp.int32)[:, None]
    col_ids = jnp.arange(length, dtype=jnp.int32)[None, :]
    valid = (col_ids >= row_ids) & (col_ids <= row_ids + span) & (col_ids >= span - offset)

    def one_head(head_index, total):
        start = head_index * ATT_DIM
        query_head = lax.dynamic_slice_in_dim(queries, start, ATT_DIM, 1)
        key_head = lax.dynamic_slice_in_dim(window_keys, start, ATT_DIM, 1)
        value_head = lax.dynamic_slice_in_dim(window_values, start, ATT_DIM, 1)
        scores = jnp.dot(query_head, key_head.T, preferred_element_type=jnp.float32) * scale
        scores = jnp.where(valid, scores, -1e30)
        highest = jnp.max(scores, axis=-1, keepdims=True)
        weights = jnp.exp(scores - highest)
        probs = (weights / jnp.sum(weights, axis=-1, keepdims=True)).astype(jnp.bfloat16)
        output = jnp.dot(probs, value_head, preferred_element_type=jnp.float32)
        return lax.dynamic_update_slice_in_dim(total, output, start, 1)

    return lax.fori_loop(0, width // ATT_DIM, one_head, jnp.zeros((rows_here, width), jnp.float32))


def local(queries, keys, values, rates, fast_gate, fast_up, fast_down):
    tokens_here = queries.shape[0]
    group_heads = fast_gate.shape[0]
    span = WINDOW - 1
    reach = (span + tokens_here - 1) // tokens_here
    earlier_keys = []
    earlier_values = []
    for distance in range(reach, 0, -1):
        count = min(tokens_here, span - (distance - 1) * tokens_here)
        moved = shifted(
            (keys[tokens_here - count :], values[tokens_here - count :]), "ctx", distance
        )
        earlier_keys.append(moved[0])
        earlier_values.append(moved[1])
    window_keys = jnp.concatenate(earlier_keys + [keys], axis=0)
    window_values = jnp.concatenate(earlier_values + [values], axis=0)
    offset = lax.axis_index("ctx") * tokens_here
    attended = window_attention(queries, window_keys, window_values, offset, span)
    stacked_weights = jnp.stack([fast_gate, fast_up, fast_down], axis=1).reshape(
        group_heads * 3 * FAST_DIM, FAST_DIM
    )
    gradients = head_gradients(keys, values, rates, fast_gate, fast_up, fast_down)
    gradients = gradients.reshape(group_heads * 3 * FAST_DIM, FAST_DIM)
    share = lax.psum_scatter(gradients, "ctx", scatter_dimension=0, tiled=True)
    share_rows = share.shape[0]
    own_weights = lax.dynamic_slice_in_dim(
        stacked_weights, lax.axis_index("ctx") * share_rows, share_rows, 0
    )
    fresh = lax.all_gather(renormalize(own_weights, share), "ctx", axis=0, tiled=True)
    fresh = fresh.reshape(group_heads, 3, FAST_DIM, FAST_DIM)
    trained = head_outputs(queries, fresh)
    return (attended + trained).astype(jnp.bfloat16)


def solution(mesh):
    in_specs = (
        P("ctx", "head"),
        P("ctx", "head"),
        P("ctx", "head"),
        P("ctx", "head"),
        P("head", None, None),
        P("head", None, None),
        P("head", None, None),
    )
    out_specs = P("ctx", "head")
    return jax.shard_map(local, mesh=mesh, in_specs=in_specs, out_specs=out_specs, check_vma=False)
```

profile of v0, /device:TPU:0, one launch (start us, length us, event | category | flops | bytes accessed | tf_op | source)
XLA Modules:
  0.0 375.3 jit_solution(7026599857273906276)
XLA Ops:
  6.5 1.7 fusion.68
  8.3 1.7 fusion.62
  10.0 1.4 fusion.70
  11.9 1.5 fusion.66
  25.6 1.4 maximum_bitcast_fusion
  26.9 1.4 maximum_bitcast_fusion.2
  28.3 5.0 %pad_maximum_fusion = f32[4,3,512,512]{3,2,1,0:T(8,128)} fusion(f32[1,3,512,512]{3,2,1,0:T(8,128)S(1)} %get-tuple-element.158, f32[1,3,512,512]{3,2,1,0:T(8,128)S(1)} %get-tuple-element.157, f32[1,3,512,512]{3,2,1,0:T(8,128)S(1)} %get-tuple-element.156, f32[1,3,512,512]{3,2,1,0:T(8,128)S(1)} %get-tuple-element.155), kind=kLoop, calls=%fused_computation.17 | loop fusion | flops 9437184 | bytes 25165824 | tf_op jit(solution)/shard_map/stack | solution.py:53
  33.7 4.3 %collective-permute-start.3 = (bf16[255,2048]{1,0:T(8,128)(2,1)S(1)}, bf16[255,2048]{1,0:T(8,128)(2,1)S(1)}, u32[]{:S(2)}, u32[]{:S(2)}) collective-permute-start(bf16[255,2048]{1,0:T(8,128)(2,1)S(1)} %slice.127), channel_id=1, source_target_pairs={{0,6},{2,8},{4,10},{6,12},{8,14},{10,16},{12,18},{14,20},{16,22},{... | collective-permute-start | bytes 3133448 | tf_op jit(solution)/shard_map/ppermute | solution.py:14
  38.0 4.7 %collective-permute-start.4 = (bf16[384,2048]{1,0:T(8,128)(2,1)S(1)}, bf16[384,2048]{1,0:T(8,128)(2,1)}, u32[]{:S(2)}, u32[]{:S(2)}) collective-permute-start(bf16[384,2048]{1,0:T(8,128)(2,1)S(1)} %copy-done.3), channel_id=1, source_target_pairs={{0,4},{2,6},{4,8},{6,10},{8,12},{10,14},{12,16},{14,18},{16,20},{1... | collective-permute-start | bytes 4718600 | tf_op jit(solution)/shard_map/ppermute | solution.py:14
  42.8 3.4 collective-permute-start.5
  46.2 2.4 collective-permute-start.1
  48.6 3.8 %collective-permute-start.2 = (bf16[384,2048]{1,0:T(8,128)(2,1)S(1)}, bf16[384,2048]{1,0:T(8,128)(2,1)}, u32[]{:S(2)}, u32[]{:S(2)}) collective-permute-start(bf16[384,2048]{1,0:T(8,128)(2,1)S(1)} %copy-done), channel_id=1, source_target_pairs={{0,2},{2,4},{4,6},{6,8},{8,10},{10,12},{12,14},{14,16},{16,18},{18... | collective-permute-start | bytes 4718600 | tf_op jit(solution)/shard_map/ppermute | solution.py:14
  53.6 4.6 %collective-permute-done.3 = bf16[255,2048]{1,0:T(8,128)(2,1)S(1)} collective-permute-done((bf16[255,2048]{1,0:T(8,128)(2,1)S(1)}, bf16[255,2048]{1,0:T(8,128)(2,1)S(1)}, u32[]{:S(2)}, u32[]{:S(2)}) %collective-permute-start.3) | collective-permute-done | bytes 1044512 | tf_op jit(solution)/shard_map/ppermute | solution.py:14
  59.2 7.5 %collective-permute-start = (bf16[255,2048]{1,0:T(8,128)(2,1)}, bf16[255,2048]{1,0:T(8,128)(2,1)}, u32[]{:S(2)}, u32[]{:S(2)}) collective-permute-start(bf16[255,2048]{1,0:T(8,128)(2,1)} %slice.126), channel_id=1, source_target_pairs={{0,6},{2,8},{4,10},{6,12},{8,14},{10,16},{12,18},{14,20},{16,22},{... | collective-permute-start | bytes 3133448 | tf_op jit(solution)/shard_map/ppermute | solution.py:14
  66.7 6.5 %pad_maximum_fusion.1 = bf16[4,3,512,512]{3,2,1,0:T(8,128)(2,1)} fusion(bf16[4,1,512,512]{3,2,1,0:T(8,128)(2,1)} %bitcast.159, bf16[4,1,512,512]{3,2,1,0:T(8,128)(2,1)} %bitcast.155, bf16[4,1,512,512]{3,2,1,0:T(8,128)(2,1)} %bitcast.156), kind=kLoop, calls=%fused_computation.18 | loop fusion | flops 6291456 | bytes 12582912 | tf_op jit(solution)/shard_map/stack | solution.py:130
  73.2 35.6 %collective-permute-done.4 = bf16[384,2048]{1,0:T(8,128)(2,1)} collective-permute-done((bf16[384,2048]{1,0:T(8,128)(2,1)S(1)}, bf16[384,2048]{1,0:T(8,128)(2,1)}, u32[]{:S(2)}, u32[]{:S(2)}) %collective-permute-start.4) | collective-permute-done | bytes 1572896 | tf_op jit(solution)/shard_map/ppermute | solution.py:14
  108.8 30.2 %concatenate.10 = bf16[1407,2048]{1,0:T(8,128)(2,1)} concatenate(bf16[255,2048]{1,0:T(8,128)(2,1)} %copy-done.6, bf16[384,2048]{1,0:T(8,128)(2,1)} %collective-permute-done.4, bf16[384,2048]{1,0:T(8,128)(2,1)} %collective-permute-done.5, bf16[384,2048]{1,0:T(8,128)(2,1)S(1)} %copy-done.3), dimensions={0} | concatenate | bytes 11526144 | tf_op jit(solution)/shard_map/concatenate | solution.py:127
  139.0 42.9 %collective-permute-done = bf16[255,2048]{1,0:T(8,128)(2,1)} collective-permute-done((bf16[255,2048]{1,0:T(8,128)(2,1)}, bf16[255,2048]{1,0:T(8,128)(2,1)}, u32[]{:S(2)}, u32[]{:S(2)}) %collective-permute-start) | collective-permute-done | bytes 1044512 | tf_op jit(solution)/shard_map/ppermute | solution.py:14
  181.9 30.1 %concatenate.9 = bf16[1407,2048]{1,0:T(8,128)(2,1)} concatenate(bf16[255,2048]{1,0:T(8,128)(2,1)} %collective-permute-done, bf16[384,2048]{1,0:T(8,128)(2,1)} %collective-permute-done.1, bf16[384,2048]{1,0:T(8,128)(2,1)} %collective-permute-done.2, bf16[384,2048]{1,0:T(8,128)(2,1)S(1)} %copy-done), dimensions={0} | concatenate | bytes 11526144 | tf_op jit(solution)/shard_map/concatenate | solution.py:126
  212.0 64.1 %reduce-scatter.2.cloned.1.call-done = f32[384,512]{1,0:T(8,128)} async-done(((f32[6144,512]{1,0:T(8,128)}), f32[384,512]{1,0:T(8,128)}) %reduce-scatter.2.cloned.1.call-update) | async-done | bytes 786448 | tf_op jit(solution)/shard_map/reduce_scatter | solution.py:135
  276.2 1.5 fusion.25
  277.7 2.1 multiply_convert_fusion
  280.2 62.4 %while.14 = (s32[]{:T(128)}, f32[384,2048]{1,0:T(8,128)S(1)}, bf16[384,2048]{1,0:T(8,128)(2,1)}, bf16[1407,2048]{1,0:T(8,128)(2,1)}, bf16[1407,2048]{1,0:T(8,128...) while((s32[]{:T(128)}, f32[384,2048]{1,0:T(8,128)S(1)}, ...), condition=%wide.region_3.4_spmd.clone, body=%wide.region_0.3_spmd.clone.sunk | while | flops 283110144 | bytes 7514650 | solution.py:109
  280.2 1.9 fusion.151
  282.5 1.6 convolution_dynamic-update-slice_fusion.2
  284.1 1.9 fusion.151
  286.4 1.6 convolution_dynamic-update-slice_fusion.2
  288.0 1.9 fusion.151
  290.3 1.6 convolution_dynamic-update-slice_fusion.2
  291.9 1.9 fusion.151
  294.2 1.6 convolution_dynamic-update-slice_fusion.2
  295.8 1.9 fusion.151
  298.1 1.6 convolution_dynamic-update-slice_fusion.2
  299.7 1.9 fusion.151
  302.0 1.6 convolution_dynamic-update-slice_fusion.2
  303.5 1.9 fusion.151
  305.8 1.6 convolution_dynamic-update-slice_fusion.2
  307.4 1.9 fusion.151
  309.7 1.6 convolution_dynamic-update-slice_fusion.2
  311.3 1.9 fusion.151
  313.6 1.6 convolution_dynamic-update-slice_fusion.2
  315.2 1.9 fusion.151
  317.5 1.6 convolution_dynamic-update-slice_fusion.2
  319.1 1.9 fusion.151
  321.4 1.6 convolution_dynamic-update-slice_fusion.2
  323.0 1.9 fusion.151
  325.3 1.6 convolution_dynamic-update-slice_fusion.2
  326.9 1.9 fusion.151
  329.2 1.6 convolution_dynamic-update-slice_fusion.2
  330.8 1.9 fusion.151
  333.1 1.6 convolution_dynamic-update-slice_fusion.2
  334.7 1.9 fusion.151
  337.0 1.6 convolution_dynamic-update-slice_fusion.2
  338.6 2.0 fusion.151
  341.0 1.6 convolution_dynamic-update-slice_fusion.2
  342.6 2.5 convolution_bitcast_fusion.19
  345.2 2.5 convolution_bitcast_fusion.17
  347.7 2.4 convolution_bitcast_fusion.15
  350.1 2.3 convolution_bitcast_fusion.13
  352.4 3.1 fusion.21
  355.6 3.1 fusion.22
  358.7 3.2 fusion.23
  361.9 3.2 fusion.24
  365.1 3.4 fusion.12
  (67 shorter events, 22.5 us)
Async XLA Ops:
  6.5 3.4 copy-start
  6.5 269.6 %reduce-scatter.2.cloned.1.call-start = ((), (), s32[]{:S(2)}) async-start(), calls=%async_computation.1 | async-start | bytes 13369344 | tf_op jit(solution)/shard_map/reduce_scatter | solution.py:135
  6.5 4.9 %copy-start.1 = (bf16[4,512,512]{2,1,0:T(8,128)(2,1)S(1)}, bf16[4,512,512]{2,1,0:T(8,128)(2,1)}, u32[]{:S(2)}) copy-start(bf16[4,512,512]{2,1,0:T(8,128)(2,1)} %param.14) | copy-start | bytes 6291460
  8.3 3.6 copy-start.7
  8.3 3.6 copy-start.3
  14.7 1.6 copy-start.4
  17.8 1.6 copy-start.2
  33.4 309.2 %all-gather.2.cloned.1.call-start = ((), (), s32[]{:S(2)}) async-start(), calls=%async_computation.2 | async-start | bytes 6684672 | tf_op jit(solution)/shard_map/all_gather | solution.py:140
  33.7 24.5 %collective-permute-start.3 = (bf16[255,2048]{1,0:T(8,128)(2,1)S(1)}, bf16[255,2048]{1,0:T(8,128)(2,1)S(1)}, u32[]{:S(2)}, u32[]{:S(2)}) collective-permute-start(bf16[255,2048]{1,0:T(8,128)(2,1)S(1)} %slice.127), channel_id=1, source_target_pairs={{0,6},{2,8},{4,10},{6,12},{8,14},{10,16},{12,18},{14,20},{16,22},{... | collective-permute-start | bytes 3133448 | tf_op jit(solution)/shard_map/ppermute | solution.py:14
  38.0 70.7 %collective-permute-start.4 = (bf16[384,2048]{1,0:T(8,128)(2,1)S(1)}, bf16[384,2048]{1,0:T(8,128)(2,1)}, u32[]{:S(2)}, u32[]{:S(2)}) collective-permute-start(bf16[384,2048]{1,0:T(8,128)(2,1)S(1)} %copy-done.3), channel_id=1, source_target_pairs={{0,4},{2,6},{4,8},{6,10},{8,12},{10,14},{12,16},{14,18},{16,20},{1... | collective-permute-start | bytes 4718600 | tf_op jit(solution)/shard_map/ppermute | solution.py:14
  42.8 66.0 %collective-permute-start.5 = (bf16[384,2048]{1,0:T(8,128)(2,1)S(1)}, bf16[384,2048]{1,0:T(8,128)(2,1)}, u32[]{:S(2)}, u32[]{:S(2)}) collective-permute-start(bf16[384,2048]{1,0:T(8,128)(2,1)S(1)} %copy-done.3), channel_id=1, source_target_pairs={{0,2},{2,4},{4,6},{6,8},{8,10},{10,12},{12,14},{14,16},{16,18},{18... | collective-permute-start | bytes 4718600 | tf_op jit(solution)/shard_map/ppermute | solution.py:14
  46.2 135.7 %collective-permute-start.1 = (bf16[384,2048]{1,0:T(8,128)(2,1)S(1)}, bf16[384,2048]{1,0:T(8,128)(2,1)}, u32[]{:S(2)}, u32[]{:S(2)}) collective-permute-start(bf16[384,2048]{1,0:T(8,128)(2,1)S(1)} %copy-done), channel_id=1, source_target_pairs={{0,4},{2,6},{4,8},{6,10},{8,12},{10,14},{12,16},{14,18},{16,20},{1... | collective-permute-start | bytes 4718600 | tf_op jit(solution)/shard_map/ppermute | solution.py:14
  48.6 133.3 %collective-permute-start.2 = (bf16[384,2048]{1,0:T(8,128)(2,1)S(1)}, bf16[384,2048]{1,0:T(8,128)(2,1)}, u32[]{:S(2)}, u32[]{:S(2)}) collective-permute-start(bf16[384,2048]{1,0:T(8,128)(2,1)S(1)} %copy-done), channel_id=1, source_target_pairs={{0,2},{2,4},{4,6},{6,8},{8,10},{10,12},{12,14},{14,16},{16,18},{18... | collective-permute-start | bytes 4718600 | tf_op jit(solution)/shard_map/ppermute | solution.py:14
  58.2 1.0 copy-start.6
  59.2 122.7 %collective-permute-start = (bf16[255,2048]{1,0:T(8,128)(2,1)}, bf16[255,2048]{1,0:T(8,128)(2,1)}, u32[]{:S(2)}, u32[]{:S(2)}) collective-permute-start(bf16[255,2048]{1,0:T(8,128)(2,1)} %slice.126), channel_id=1, source_target_pairs={{0,6},{2,8},{4,10},{6,12},{8,14},{10,16},{12,18},{14,20},{16,22},{... | collective-permute-start | bytes 3133448 | tf_op jit(solution)/shard_map/ppermute | solution.py:14
  342.6 5.1 %copy-start.5 = (bf16[384,2048]{1,0:T(8,128)(2,1)S(1)}, bf16[384,2048]{1,0:T(8,128)(2,1)}, u32[]{:S(2)}) copy-start(bf16[384,2048]{1,0:T(8,128)(2,1)} %get-tuple-element.250) | copy-start | bytes 4718596
Sparse Core Ops, SparseCore 0:
  33.5 242.5 reduce-scatter.1
  279.9 60.9 all-gather.1
where the time goes:
time: 379 us; the launch traced here: 375 us
  waiting for transfers between devices  147 us (39%)
  matrix products  94.1 us (25%)
  local copies, waits for them, and re-layouts  65.2 us (17%)
  other arithmetic  28.4 us (7%)
  starting transfers between devices  26.2 us (7%)
  between operations  13.7 us (4%)
    ppermute x6, waiting for transfers between devices, shifted(): return lax.ppermute(value, axis, pairs)  83.1 us
    reduce_scatter x1, waiting for transfers between devices, local(): share = lax.psum_scatter(gradients, 'ctx', scatter_dimension=0, tiled=True)  64.1 us
    concatenate x1, local copies, waits for them, and re-layouts, local(): window_values = jnp.concatenate(earlier_values + [values], axis=0)  30.2 us
    concatenate x1, local copies, waits for them, and re-layouts, local(): window_keys = jnp.concatenate(earlier_keys + [keys], axis=0)  30.1 us
    dot_general x16, matrix products, one_head(): jnp.dot(query_head, key_head.T, preferred_element_type=jnp.float32) * scale  30 us
    ppermute x6, starting transfers between devices, shifted(): return lax.ppermute(value, axis, pairs)  26.2 us
    dot_general x16, matrix products, one_head(): output = jnp.dot(probs, value_head, preferred_element_type=jnp.float32)  24.9 us
    dot_general x4, matrix products, apply_fast(): return jnp.dot(applied, downward.T, preferred_element_type=jnp.float32)  12.7 us
  transfers between devices with their start and end apart: 8, of which 4 were waited for; matrix products, arithmetic and copies ran while one was open for 35% of the time, Pallas kernels for 0%

commit v1 on v0

v1 whole, which is shorter than its diff:
```python
import functools
import math

import jax
import jax.numpy as jnp
from jax import lax
from jax.experimental import pallas as pl
from jax.experimental.pallas import tpu as pltpu
from jax.sharding import PartitionSpec as P

ATT_DIM = 128
FAST_DIM = 512
WINDOW = 1024
F32 = jnp.float32
BF16 = jnp.bfloat16
COEF = math.log2(math.e) / math.sqrt(ATT_DIM)


def dot_nt(a, b):
    return lax.dot_general(a, b, (((1,), (1,)), ((), ())), preferred_element_type=F32)


def dot_tn(a, b):
    return lax.dot_general(a, b, (((0,), (0,)), ((), ())), preferred_element_type=F32)


def dot_nn(a, b):
    return lax.dot_general(a, b, (((1,), (0,)), ((), ())), preferred_element_type=F32)


def kernel(
    n, orders, q_hbm, k_hbm, v_hbm, rates_ref, gate_hbm, up_hbm, down_hbm, out_ref,
    kwin, vwin, qbuf, wbuf, gsend, grecv, acc, sbuf, rbuf, fresh, lse, oacc,
    load_sem, kv_send, kv_recv, core_send, core_recv,
    rs_send, rs_recv, ag_send, ag_recv, fw_send, fw_recv,
):
    me = lax.axis_index("ctx")
    tok = qbuf.shape[0]
    halo = WINDOW
    tail = halo - 2 * tok
    heads = qbuf.shape[1] // ATT_DIM
    rows = acc.shape[1]
    steps = len(orders[0])
    core = lax.rem(me, 2)
    sibling = me + 1 - 2 * core

    def bit_of(b):
        return lax.rem(lax.div(me, 1 << b), 2)

    def partner(b):
        return me + (1 - 2 * bit_of(b)) * (1 << b)

    own = pl.ds(halo, tok)
    loads = [
        pltpu.make_async_copy(k_hbm, kwin.at[own], load_sem.at[0]),
        pltpu.make_async_copy(v_hbm, vwin.at[own], load_sem.at[1]),
        pltpu.make_async_copy(gate_hbm, wbuf.at[:, pl.ds(0 * FAST_DIM, FAST_DIM)], load_sem.at[2]),
        pltpu.make_async_copy(up_hbm, wbuf.at[:, pl.ds(1 * FAST_DIM, FAST_DIM)], load_sem.at[3]),
        pltpu.make_async_copy(down_hbm, wbuf.at[:, pl.ds(2 * FAST_DIM, FAST_DIM)], load_sem.at[4]),
        pltpu.make_async_copy(q_hbm, qbuf, load_sem.at[5]),
    ]
    for load in loads:
        load.start()

    barrier = pltpu.get_barrier_semaphore()
    greeted = [partner(b) for b in range(steps + 1)]
    for shift in (2, n - 2, 3, n - 3):
        greeted.append(lax.rem(me + shift, n))
    for other in greeted:
        pl.semaphore_signal(
            barrier, inc=1, device_id={"ctx": other}, device_id_type=pl.DeviceIdType.MESH
        )
    pl.semaphore_wait(barrier, len(greeted))

    def remote(src, dst, send, recv, to):
        return pltpu.make_async_remote_copy(
            src_ref=src, dst_ref=dst, send_sem=send, recv_sem=recv,
            device_id={"ctx": to}, device_id_type=pl.DeviceIdType.MESH,
        )

    last = pl.ds(halo + tok - tail, tail)
    far = pl.ds(0, tail)
    mid = pl.ds(tail, tok)
    near = pl.ds(tail + tok, tok)

    def pair(src, dst, lane, to):
        return [
            remote(win.at[src], win.at[dst], kv_send.at[lane, w], kv_recv.at[lane, w], to)
            for w, win in enumerate((kwin, vwin))
        ]

    two = pair(own, mid, 0, lax.rem(me + 2, n))
    near_own = pair(own, near, 1, sibling)
    three = pair(last, far, 2, lax.rem(me + 3, n))
    near_pass = pair(mid, near, 1, sibling)
    far_pass = pair(pl.ds(tail + tok - tail, tail), far, 2, sibling)

    loads[0].wait()
    loads[1].wait()

    def begin(copies):
        for copy in copies:
            copy.start()

    @pl.when(me + 2 < n)
    def _():
        begin(two)

    @pl.when(core == 0)
    def _():
        begin(near_own)

    @pl.when((core == 1) & (me + 3 < n))
    def _():
        begin(three)

    zero_far = jnp.zeros((tail, kwin.shape[1]), BF16)
    zero_tok = jnp.zeros((tok, kwin.shape[1]), BF16)

    @pl.when(me < 3)
    def _():
        kwin[far] = zero_far
        vwin[far] = zero_far

    @pl.when(me < 2)
    def _():
        kwin[mid] = zero_tok
        vwin[mid] = zero_tok

    @pl.when(me < 1)
    def _():
        kwin[near] = zero_tok
        vwin[near] = zero_tok

    for load in loads[2:5]:
        load.wait()

    lane_ids = lax.broadcasted_iota(jnp.int32, rates_ref.shape, 1)

    def gradients(head, store):
        cols = pl.ds(pl.multiple_of(head * FAST_DIM, FAST_DIM), FAST_DIM)
        keys = kwin[own, cols]
        rate = jnp.sum(
            jnp.where(lane_ids == head, rates_ref[...].astype(F32), 0.0), axis=1, keepdims=True
        )
        out_grad = (-rate * vwin[own, cols].astype(F32)).astype(BF16)
        gate_pre = dot_nt(keys, wbuf[head, pl.ds(0 * FAST_DIM, FAST_DIM), :])
        up_pre = dot_nt(keys, wbuf[head, pl.ds(1 * FAST_DIM, FAST_DIM), :])
        sig = jax.nn.sigmoid(gate_pre)
        act = gate_pre * sig
        hidden = (act * up_pre).astype(BF16)
        hidden_grad = dot_nn(out_grad, wbuf[head, pl.ds(2 * FAST_DIM, FAST_DIM), :])
        gate_grad = (hidden_grad * up_pre * (sig * (1.0 + gate_pre * (1.0 - sig)))).astype(BF16)
        up_grad = (hidden_grad * act).astype(BF16)
        store(0, dot_tn(gate_grad, keys))
        store(1, dot_tn(up_grad, keys))
        store(2, dot_tn(out_grad, hidden))

    core_copies = [
        remote(gsend.at[j], grecv.at[j], core_send.at[j], core_recv.at[j], sibling)
        for j in range(2)
    ]
    for j in range(2):

        def store_send(m, value, j=j):
            gsend[j, pl.ds(m * FAST_DIM, FAST_DIM), :] = value.astype(BF16)

        gradients((1 - core) * 2 + j, store_send)
        core_copies[j].start()

    start = [jnp.int32(0), jnp.int32(0)]
    spans = [[], []]
    rs_copies = [[], []]

    def slot(k):
        return rows - (rows >> k)

    def halve(j, k):
        size = rows >> k
        half = size // 2
        b = orders[j][k]
        bit = bit_of(b)
        pending = grecv.at[j] if k == 0 else rbuf.at[j, pl.ds(slot(k - 1), size)]
        base = start[j]
        spans[j].append((base, size))

        def at(ref, first):
            return ref[pl.ds(pl.multiple_of(first, 16), half), :]

        give = (1 - bit) * half
        keep = bit * half
        acc_j = acc.at[j]
        place = pl.ds(slot(k), half)
        sbuf[j, place, :] = (at(acc_j, base + give) + at(pending, give).astype(F32)).astype(BF16)
        copy = remote(
            sbuf.at[j, place], rbuf.at[j, place], rs_send.at[j, k], rs_recv.at[j, k], partner(b)
        )
        copy.start()
        rs_copies[j].append(copy)
        acc[j, pl.ds(pl.multiple_of(base + keep, 16), half), :] = at(acc_j, base + keep) + at(
            pending, keep
        ).astype(F32)
        start[j] = base + keep

    for j in range(2):

        def store_acc(m, value, j=j):
            acc[j, pl.ds(m * FAST_DIM, FAST_DIM), :] = value

        gradients(core * 2 + j, store_acc)
        core_copies[j].wait()
        halve(j, 0)

    loads[5].wait()

    row_ids = lax.broadcasted_iota(jnp.int32, (tok, tok), 0)
    col_ids = lax.broadcasted_iota(jnp.int32, (tok, tok), 1)

    def own_block(a, carry):
        cols = pl.ds(pl.multiple_of(a * ATT_DIM, ATT_DIM), ATT_DIM)
        scores = dot_nt(qbuf[:, cols], kwin[own, cols]) * COEF
        scores = jnp.where(col_ids <= row_ids, scores, -1e30)
        top = jnp.max(scores, axis=1, keepdims=True)
        probs = jnp.exp2(scores - top)
        total = jnp.sum(probs, axis=1, keepdims=True)
        oacc[:, cols] = dot_nn(probs.astype(BF16), vwin[own, cols]) / total
        lse[a] = jnp.broadcast_to(top + jnp.log2(total), (tok, ATT_DIM))
        return carry

    first_key = halo - me * tok
    past = lax.broadcasted_iota(jnp.int32, (1, halo), 1)
    bias = jnp.where(past >= first_key, 0.0, -1e30).astype(F32)

    def halo_block(a, carry):
        cols = pl.ds(pl.multiple_of(a * ATT_DIM, ATT_DIM), ATT_DIM)
        q = qbuf[:, cols]
        edge = dot_nt(q, kwin[pl.ds(0, tok), cols]) * COEF + bias[:, :tok]
        edge = jnp.where(col_ids > row_ids, edge, -1e30)
        rest = dot_nt(q, kwin[pl.ds(tok, halo - tok), cols]) * COEF + bias[:, tok:]
        before = lse[a][:, :1]
        top = jnp.maximum(
            jnp.maximum(jnp.max(edge, axis=1, keepdims=True), jnp.max(rest, axis=1, keepdims=True)),
            before,
        )
        p_edge = jnp.exp2(edge - top)
        p_rest = jnp.exp2(rest - top)
        kept = jnp.exp2(before - top)
        total = (
            kept + jnp.sum(p_edge, axis=1, keepdims=True) + jnp.sum(p_rest, axis=1, keepdims=True)
        )
        mixed = dot_nn(p_edge.astype(BF16), vwin[pl.ds(0, tok), cols]) + dot_nn(
            p_rest.astype(BF16), vwin[pl.ds(tok, halo - tok), cols]
        )
        oacc[:, cols] = (mixed + kept * oacc[:, cols]) / total
        return carry

    cuts = [heads * i // steps for i in range(steps + 1)]
    for k in range(steps):
        lax.fori_loop(cuts[k], cuts[k + 1], own_block, 0)
        if k == 0:
            @pl.when(me >= 2)
            def _():
                for copy in two:
                    copy.wait_recv()

            @pl.when((me >= 2) & (core == 1))
            def _():
                begin(near_pass)

            @pl.when((me >= 2) & (core == 0))
            def _():
                begin(far_pass)

        for j in range(2):
            rs_copies[j][k].wait()
            if k + 1 < steps:
                halve(j, k + 1)

    size = rows >> steps
    ag_copies = [[], []]
    fw_copies = [[], []]

    def forward(j, first, length, index):
        place = pl.ds(pl.multiple_of(first, 16), length)
        copy = remote(
            fresh.at[core * 2 + j, place], fresh.at[core * 2 + j, place],
            fw_send.at[j, index], fw_recv.at[j, index], sibling,
        )
        copy.start()
        arrive = remote(
            fresh.at[core * 2 + j, place], fresh.at[(1 - core) * 2 + j, place],
            fw_send.at[j, index], fw_recv.at[j, index], sibling,
        )
        fw_copies[j].append((copy, arrive))

    def gather(j, k):
        base, length = spans[j][k + 1] if k + 1 < steps else (start[j], size)
        place = pl.ds(pl.multiple_of(base, 16), length)
        copy = remote(
            fresh.at[core * 2 + j, place], fresh.at[core * 2 + j, place],
            ag_send.at[j, k], ag_recv.at[j, k], partner(orders[j][k]),
        )
        copy.start()
        parent = spans[j][k][0]
        incoming = parent + parent + length - base
        arrive = remote(
            fresh.at[core * 2 + j, place],
            fresh.at[core * 2 + j, pl.ds(pl.multiple_of(incoming, 16), length)],
            ag_send.at[j, k], ag_recv.at[j, k], partner(orders[j][k]),
        )
        ag_copies[j].append((copy, arrive, incoming, length))

    for j in range(2):
        place = pl.ds(pl.multiple_of(start[j], 16), size)
        grad = acc[j, place, :] + rbuf[j, pl.ds(slot(steps - 1), size), :].astype(F32)
        initial = wbuf[core * 2 + j, place, :].astype(F32)
        moved = initial - grad
        target = jnp.sqrt(jnp.sum(initial * initial, axis=1, keepdims=True))
        current = jnp.sqrt(jnp.sum(moved * moved, axis=1, keepdims=True) + 1e-06)
        fresh[core * 2 + j, place, :] = (moved * (target / current)).astype(BF16)
        gather(j, steps - 1)
        forward(j, start[j], size, 0)

    @pl.when(me >= 1)
    def _():
        for copy in near_own:
            copy.wait_recv()

    @pl.when(me >= 3)
    def _():
        for copy in three:
            copy.wait_recv()

    cuts = [heads * i // steps for i in range(steps + 1)]
    for i in range(steps):
        lax.fori_loop(cuts[i], cuts[i + 1], halo_block, 0)
        k = steps - 1 - i
        for j in range(2):
            copy, arrive, incoming, length = ag_copies[j][i]
            arrive.wait_recv()
            if k > 0:
                gather(j, k - 1)
            forward(j, incoming, length, i + 1)

    def apply(head):
        cols = pl.ds(pl.multiple_of(head * FAST_DIM, FAST_DIM), FAST_DIM)
        q = qbuf[:, cols]
        gate_pre = dot_nt(q, fresh[head, pl.ds(0, FAST_DIM), :])
        up_pre = dot_nt(q, fresh[head, pl.ds(FAST_DIM, FAST_DIM), :])
        applied = (gate_pre * jax.nn.sigmoid(gate_pre) * up_pre).astype(BF16)
        trained = dot_nt(applied, fresh[head, pl.ds(2 * FAST_DIM, FAST_DIM), :])
        out_ref[:, cols] = (oacc[:, cols] + trained).astype(BF16)

    for j in range(2):
        apply(core * 2 + j)
    for j in range(2):
        for copy, arrive in fw_copies[j]:
            arrive.wait_recv()
        apply((1 - core) * 2 + j)

    for j in range(2):
        for copy, arrive, incoming, length in ag_copies[j]:
            copy.wait_send()
        for copy, arrive in fw_copies[j]:
            copy.wait_send()

    def drain(copies):
        for copy in copies:
            copy.wait_send()

    @pl.when(me + 2 < n)
    def _():
        drain(two)

    @pl.when(core == 0)
    def _():
        drain(near_own)

    @pl.when((core == 1) & (me + 3 < n))
    def _():
        drain(three)

    @pl.when((me >= 2) & (core == 1))
    def _():
        drain(near_pass)

    @pl.when((me >= 2) & (core == 0))
    def _():
        drain(far_pass)


def local(n, orders, queries, keys, values, rates, fast_gate, fast_up, fast_down):
    tok, width = queries.shape
    group = fast_gate.shape[0]
    rows = 3 * FAST_DIM
    steps = len(orders[0])
    dma = pltpu.SemaphoreType.DMA
    hbm = pl.BlockSpec(memory_space=pl.ANY)
    vmem = pl.BlockSpec(memory_space=pltpu.VMEM)
    return pl.pallas_call(
        functools.partial(kernel, n, orders),
        out_shape=jax.ShapeDtypeStruct((tok, width), BF16),
        in_specs=[hbm, hbm, hbm, vmem, hbm, hbm, hbm],
        out_specs=vmem,
        scratch_shapes=[
            pltpu.VMEM((WINDOW + tok, width), BF16),
            pltpu.VMEM((WINDOW + tok, width), BF16),
            pltpu.VMEM((tok, width), BF16),
            pltpu.VMEM((group, rows, FAST_DIM), BF16),
            pltpu.VMEM((2, rows, FAST_DIM), BF16),
            pltpu.VMEM((2, rows, FAST_DIM), BF16),
            pltpu.VMEM((2, rows, FAST_DIM), F32),
            pltpu.VMEM((2, rows, FAST_DIM), BF16),
            pltpu.VMEM((2, rows, FAST_DIM), BF16),
            pltpu.VMEM((group, rows, FAST_DIM), BF16),
            pltpu.VMEM((width // ATT_DIM, tok, ATT_DIM), F32),
            pltpu.VMEM((tok, width), F32),
            dma((6,)),
            dma((3, 2)),
            dma((3, 2)),
            dma((2,)),
            dma((2,)),
            dma((2, steps)),
            dma((2, steps)),
            dma((2, steps)),
            dma((2, steps)),
            dma((2, steps + 1)),
            dma((2, steps + 1)),
        ],
        compiler_params=pltpu.CompilerParams(
            collective_id=0, has_side_effects=True, vmem_limit_bytes=63 * 1024 * 1024
        ),
        cost_estimate=pl.CostEstimate(
            flops=12_000_000_000, bytes_accessed=14_000_000, transcendentals=10_000_000
        ),
    )(queries, keys, values, rates, fast_gate, fast_up, fast_down)


def solution(mesh):
    n = mesh.shape["ctx"]
    bits = n.bit_length() - 1
    order = list(range(1, bits))
    orders = (tuple(order), tuple(order[1:2] + order[:1] + order[2:]))
    in_specs = (P("ctx", "head"),) * 4 + (P("head", None, None),) * 3
    return jax.shard_map(
        functools.partial(local, n, orders),
        mesh=mesh,
        in_specs=in_specs,
        out_specs=P("ctx", "head"),
        check_vma=False,
    )
```

time: 379 us -> 180 us (0.47)
  Pallas kernels: 0 us -> 175 us
  waiting for transfers between devices: 147 us -> 0 us
  matrix products: 94.1 us -> 0 us
  local copies, waits for them, and re-layouts: 65.2 us -> 4.21 us
  other arithmetic: 28.4 us -> 0 us
  starting transfers between devices: 26.2 us -> 0 us
  between operations: 13.7 us -> 0.01 us
    pallas_call x0 -> x1, Pallas kernels: none -> 175 us  [local(): pl.pallas_call(functools.partial(kernel, n, orders), out_shape=jax.ShapeD...]
    dot_general x64 -> x0, matrix products: 94.1 us -> none  [the longest x16 30 us: one_head(): jnp.dot(query_head, key_head.T, preferred_element_type=jnp.float32) * scale]
    ppermute x6 -> x0, waiting for transfers between devices: 83.1 us -> none  [shifted(): return lax.ppermute(value, axis, pairs)]
    reduce_scatter x1 -> x0, waiting for transfers between devices: 64.1 us -> none  [local(): share = lax.psum_scatter(gradients, 'ctx', scatter_dimension=0, tiled=True)]
    concatenate x2 -> x0, local copies, waits for them, and re-layouts: 60.3 us -> none  [the longest x1 30.2 us: local(): window_values = jnp.concatenate(earlier_values + [values], axis=0)]
    ppermute x6 -> x0, starting transfers between devices: 26.2 us -> none  [shifted(): return lax.ppermute(value, axis, pairs)]
    another operation x4 -> x0, other arithmetic: 14.3 us -> none  [the longest x3 7.81 us: head_gradients(): return jnp.stack(results)]
    reduce_sum x17 -> x0, other arithmetic: 8.55 us -> none  [the longest x16 7.07 us: one_head(): jnp.sum(weights, axis=-1, keepdims=True)]
  transfers between devices with their start and end apart: 8 -> 0, of which waited for: 4 -> 0; matrix products, arithmetic and copies ran while one was open for 35% -> 0% of each run, Pallas kernels for 0% -> 0%
where the time goes in v1:
time: 180 us; the launch traced here: 179 us
  Pallas kernels  175 us (97%)
  local copies, waits for them, and re-layouts  4.21 us (2%)
    pallas_call x1, Pallas kernels, local(): pl.pallas_call(functools.partial(kernel, n, orders), out_shape=jax.ShapeD...  175 us
    unnamed x2, local copies, waits for them, and re-layouts  4.21 us

profile of v1, /device:TPU:0, one launch (start us, length us, event | category | flops | bytes accessed | tf_op | source)
XLA Modules:
  0.0 179.1 jit_solution(9560053243139996550)
XLA Ops:
  0.0 1.5 copy.8.rates_ref
  1.5 174.8 %shard_map.73 = bf16[384,2048]{1,0:T(8,128)(2,1)} custom-call(bf16[384,2048]{1,0:T(8,128)(2,1)} %q_hbm.1, bf16[384,2048]{1,0:T(8,128)(2,1)} %k_hbm.1, bf16[384,2048]{1,0:T(8,128)(2,1)} %v_hbm.1, bf16[384,4]{1,0:T(8,128)(2,1)} %copy.8.rates_ref, bf16[4,512,512]{2,1,0:T(8,128)(2,1)} %gate_hbm.1, bf16[4,512,512]{2,1,0:T(8,128)(2,1)} %up_hbm.1, ...), custom_call_target="tpu_custom_call" | custom-call | flops 12000000000 | bytes 14000000 | tf_op jit(solution)/shard_map/pallas_call | solution.py:400
  176.3 2.7 %copy.10 = bf16[384,2048]{1,0:T(8,128)(2,1)} copy(bf16[384,2048]{1,0:T(8,128)(2,1)} %shard_map.73) | data formatting | bytes 3145728
